TPU v7x, 256 devices: a whole 4x4x8 slice. The times are simulated.
256 devices in a mesh: grp: 32 (over z_lo, x, core), tp: 8 (over y, z_hi).
Axes of the slice: x: 4, y: 4, z: 8 (z_hi: 2, z_lo: 4; z = z_hi * 4 + z_lo), core: 2. Of those that a mesh axis runs over, the one named last changes fastest.
Arguments:
- q_attn: bfloat16 [64, 64, 4096], P('grp', None, 'tp'), may hold values from -6 to 6
- q_resid: bfloat16 [64, 64, 4096], P('grp', None, 'tp'), may hold values from -6 to 6
- p_attn: bfloat16 [64, 128, 4096], P('grp', None, 'tp'), may hold values from -6 to 6
- p_resid: bfloat16 [64, 128, 4096], P('grp', None, 'tp'), may hold values from -6 to 6
- w_out: bfloat16 [4096, 4096], P('grp', 'tp'), may hold values from -0.09375 to 0.09375
- w_snap: bfloat16 [4096, 4096], P('grp', 'tp'), may hold values from -0.09375 to 0.09375
- norm_gain: bfloat16 [4096], P('tp'), may hold values from 0.25 to 4
- pass_attn: bfloat16 [64, 256, 4096], P('grp', None, 'tp'), may hold values from -6 to 6
- pass_resid: bfloat16 [64, 256, 4096], P('grp', None, 'tp'), may hold values from -6 to 6
- pass_len: int32 [64], P('grp'), may hold values from 128 to 256, as said below
- block_owner: int32 [32], replicated, may hold values from 0 to 31, each once
- neg_ids: int32 [64, 8], P('grp'), may hold values from 0 to 63
Outputs:
- loss: float32 [], replicated
- w_grad: float32 [4096, 4096], P('grp', 'tp')
- passage_index: bfloat16 [64, 4096], P('grp', 'tp')
Inputs may be any that keep to these rules, and one draw needn't show every extreme that they name: `pass_len`: lengths are multiples of 128; in every block of 2 slots one passage has 256 tokens.
All inputs are finite; a program needn't handle non-finite values.
Results may differ from a plain program's by a relative error of at most 0.0034.
Values may be sent and summed in bfloat16 or wider, within the bound.
A program may use at most 64 MiB of HBM per device.

v0:
```python
import jax
import jax.numpy as jnp
from jax import lax
from jax.sharding import PartitionSpec as P

EPS = 1e-06
TEMP = 0.05


def add_block(tokens, piece):
    return jnp.dot(tokens, piece, preferred_element_type=jnp.float32)


def token_norm(hidden, squares, width, gain):
    factor = lax.rsqrt(squares[:, None] / width + EPS)
    return (factor, hidden * factor * gain[None, :])


def contract_rows(left, right):
    return lax.dot_general(
        left, right, (((0,), (0,)), ((), ())), preferred_element_type=jnp.float32
    )


def spread_tokens(values, count):
    seqs, cols = values.shape
    return jnp.broadcast_to(values[:, None, :], (seqs, count, cols)).reshape(seqs * count, cols)


def shards(
    q_attn,
    q_resid,
    p_attn,
    p_resid,
    w_out,
    w_snap,
    norm_gain,
    pass_attn,
    pass_resid,
    pass_len,
    block_owner,
    neg_ids,
):
    precise = lax.Precision.HIGHEST
    grp_size = lax.axis_size("grp")
    queries, qlen, cols = q_attn.shape
    width = cols * lax.axis_size("tp")
    poslen = p_attn.shape[1]
    blocks, plen = (pass_attn.shape[0], pass_attn.shape[1])
    gain = norm_gain.astype(jnp.float32)
    pass_full = lax.all_gather(pass_attn, "tp", axis=2, tiled=True).reshape(blocks * plen, width)
    query_full, pos_full = (
        lax.all_gather(q_attn, "tp", axis=2, tiled=True),
        lax.all_gather(p_attn, "tp", axis=2, tiled=True),
    )
    query_full = query_full.reshape(queries * qlen, width)
    pos_full = pos_full.reshape(queries * poslen, width)
    proj_s = add_block(pass_full, lax.all_gather(w_snap, "grp", axis=0, tiled=True))
    piece = lax.all_gather(w_out, "grp", axis=0, tiled=True)
    proj_q = add_block(query_full, piece)
    proj_p = add_block(pos_full, piece)
    hidden_s = pass_resid.reshape(blocks * plen, cols).astype(jnp.float32) + proj_s
    squares_s = lax.psum(jnp.sum(hidden_s * hidden_s, axis=1), "tp")
    factor_s, out_s = token_norm(hidden_s, squares_s, width, gain)
    mask = (lax.broadcasted_iota(jnp.int32, (blocks, plen), 1) < pass_len[:, None]).astype(
        jnp.float32
    )
    pooled_s = jnp.sum(out_s.reshape(blocks, plen, cols) * mask[:, :, None], axis=1) / pass_len[
        :, None
    ].astype(jnp.float32)
    pool_sq = lax.psum(jnp.sum(pooled_s * pooled_s, axis=1), "tp")
    passage_index = (pooled_s * lax.rsqrt(pool_sq[:, None] / width + EPS)).astype(jnp.bfloat16)
    hidden_q = q_resid.reshape(queries * qlen, cols).astype(jnp.float32) + proj_q
    hidden_p = p_resid.reshape(queries * poslen, cols).astype(jnp.float32) + proj_p
    squares_q, squares_p = lax.psum(
        (jnp.sum(hidden_q * hidden_q, axis=1), jnp.sum(hidden_p * hidden_p, axis=1)), "tp"
    )
    factor_q, out_q = token_norm(hidden_q, squares_q, width, gain)
    factor_p, out_p = token_norm(hidden_p, squares_p, width, gain)
    pooled_q = jnp.mean(out_q.reshape(queries, qlen, cols), axis=1)
    pooled_p = jnp.mean(out_p.reshape(queries, poslen, cols), axis=1)
    index_all = lax.all_gather(passage_index, "grp", axis=0, tiled=True)
    owners = block_owner.shape[0]
    match = (neg_ids // blocks)[:, :, None] == lax.broadcasted_iota(jnp.int32, (1, 1, owners), 2)
    owner_of = jnp.sum(jnp.where(match, block_owner[None, None, :], 0), axis=2)
    slots = owner_of * blocks + neg_ids % blocks
    neg_rows = index_all[slots].astype(jnp.float32)
    sq_q, sq_p = lax.psum(
        (jnp.sum(pooled_q * pooled_q, axis=1), jnp.sum(pooled_p * pooled_p, axis=1)), "tp"
    )
    norm_q = lax.rsqrt(sq_q / width + EPS)
    norm_p = lax.rsqrt(sq_p / width + EPS)
    emb_q = pooled_q * norm_q[:, None]
    emb_p = pooled_p * norm_p[:, None]
    pos, neg = lax.psum(
        (
            jnp.sum(emb_q * emb_p, axis=1),
            jnp.einsum("qc,qjc->qj", emb_q, neg_rows, precision=precise),
        ),
        "tp",
    )
    scale = 1.0 / (width * TEMP)
    exp_pos = jnp.exp(pos * scale)
    exp_neg = jnp.exp(neg * scale)
    total = exp_pos + jnp.sum(exp_neg, axis=1)
    terms = jnp.log(total) - pos * scale
    loss = lax.psum(jnp.sum(terms), "grp") / (queries * grp_size)
    d_pos = exp_pos / total - 1.0
    d_neg = exp_neg / total[:, None]
    grad_q = (
        d_pos[:, None] * emb_p + jnp.einsum("qj,qjc->qc", d_neg, neg_rows, precision=precise)
    ) * scale
    grad_p = d_pos[:, None] * emb_q * scale
    back_q, back_p = lax.psum(
        (jnp.sum(emb_q * grad_q, axis=1), jnp.sum(emb_p * grad_p, axis=1)), "tp"
    )
    seq_q = norm_q[:, None] * (grad_q - emb_q * back_q[:, None] / width)
    seq_p = norm_p[:, None] * (grad_p - emb_p * back_p[:, None] / width)
    upper_q = spread_tokens(seq_q / qlen * gain[None, :], qlen)
    upper_p = spread_tokens(seq_p / poslen * gain[None, :], poslen)
    normed_q = hidden_q * factor_q
    normed_p = hidden_p * factor_p
    inner_q, inner_p = lax.psum(
        (jnp.sum(normed_q * upper_q, axis=1), jnp.sum(normed_p * upper_p, axis=1)), "tp"
    )
    dh_q = (factor_q * (upper_q - normed_q * inner_q[:, None] / width)).astype(jnp.bfloat16)
    dh_p = (factor_p * (upper_p - normed_p * inner_p[:, None] / width)).astype(jnp.bfloat16)
    w_grad = lax.psum_scatter(
        contract_rows(query_full, dh_q) + contract_rows(pos_full, dh_p),
        "grp",
        scatter_dimension=0,
        tiled=True,
    )
    return (loss, w_grad, passage_index)


def solution(mesh):
    placed = (
        P("grp", None, "tp"),
        P("grp", None, "tp"),
        P("grp", None, "tp"),
        P("grp", None, "tp"),
        P("grp", "tp"),
        P("grp", "tp"),
        P("tp"),
        P("grp", None, "tp"),
        P("grp", None, "tp"),
        P("grp"),
        P(),
        P("grp", None),
    )
    return jax.shard_map(
        shards,
        mesh=mesh,
        in_specs=placed,
        out_specs=(P(), P("grp", "tp"), P("grp", "tp")),
        check_vma=False,
    )
```

profile of v0, /device:TPU:24, one launch (start us, length us, event | category | flops | bytes accessed | tf_op | source)
XLA Modules:
  0.0 736.5 jit_solution(12068333558267169497)
XLA Ops:
  8.0 0.7 all-gather.9.cloned.1.call-update
  11.9 0.7 and_select_fusion.1
  12.6 0.9 select_reduce_fusion
  13.5 0.7 compare_select_fusion
  14.3 0.7 compare_convert_fusion
  15.7 58.9 %all-gather.7.cloned.1.call-done = bf16[2,64,4096]{2,1,0:T(8,128)(2,1)} async-done(((bf16[2,64,512]{2,1,0:T(8,128)(2,1)}), bf16[2,64,4096]{2,1,0:T(8,128)(2,1)}) %all-gather.7.cloned.1.call-update) | async-done | bytes 1048592 | tf_op jit(solution)/shard_map/all_gather | solution.py:53
  74.6 60.8 %all-gather.9.cloned.1.call-done = bf16[4096,512]{1,0:T(8,128)(2,1)} async-done(((bf16[128,512]{1,0:T(8,128)(2,1)}), bf16[4096,512]{1,0:T(8,128)(2,1)}) %all-gather.9.cloned.1.call-update) | async-done | bytes 4194320 | tf_op jit(solution)/shard_map/all_gather | solution.py:59
  135.4 3.3 multiply_reduce_fusion.3
  138.7 74.5 %all-gather.11.cloned.1.call-done = bf16[2,128,4096]{2,1,0:T(8,128)(2,1)} async-done(((bf16[2,128,512]{2,1,0:T(8,128)(2,1)}), bf16[2,128,4096]{2,1,0:T(8,128)(2,1)}) %all-gather.11.cloned.1.call-update) | async-done | bytes 2097168 | tf_op jit(solution)/shard_map/all_gather | solution.py:54
  213.2 4.2 multiply_reduce_fusion.2
  217.3 105.9 %all-gather.13.cloned.1.call-done = bf16[2,256,4096]{2,1,0:T(8,128)(2,1)} async-done(((bf16[2,256,512]{2,1,0:T(8,128)(2,1)}), bf16[2,256,4096]{2,1,0:T(8,128)(2,1)}) %all-gather.13.cloned.1.call-update) | async-done | bytes 4194320 | tf_op jit(solution)/shard_map/all_gather | solution.py:51
  323.2 60.6 %all-gather.15.cloned.1.call-done = bf16[4096,512]{1,0:T(8,128)(2,1)} async-done(((bf16[128,512]{1,0:T(8,128)(2,1)}), bf16[4096,512]{1,0:T(8,128)(2,1)}) %all-gather.15.cloned.1.call-update) | async-done | bytes 4194320 | tf_op jit(solution)/shard_map/all_gather | solution.py:58
  383.9 5.9 multiply_reduce_fusion.1
  389.8 27.1 %all-reduce.4 = (f32[256]{0:T(256)S(1)}, f32[128]{0:T(128)S(1)}, f32[512]{0:T(512)S(1)}) all-reduce(f32[256]{0:T(256)S(1)} %get-tuple-element.42, f32[128]{0:T(128)S(1)} %get-tuple-element.44, f32[512]{0:T(512)S(1)} %get-tuple-element.46), channel_id=1, replica_groups=mesh['grp'=32,'tp'=8] {'tp'}, use_global_device_ids=true, to_apply=%region_6.0 | all-reduce | flops 896 | bytes 7168 | tf_op jit(solution)/shard_map/psum | solution.py:75
  417.8 24.8 %all-reduce.3 = (f32[2]{0:T(128)S(1)}, f32[2]{0:T(128)S(1)}, f32[2]{0:T(128)S(1)}) all-reduce(f32[2]{0:T(128)S(1)} %multiply_reduce_fusion.8, f32[2]{0:T(128)S(1)} %multiply_reduce_fusion.9, f32[2]{0:T(128)S(1)} %get-tuple-element.27), channel_id=1, replica_groups=mesh['grp'=32,'tp'=8] {'tp'}, use_global_device_ids=true, to_apply=%region_9.0 | all-reduce | flops 6 | bytes 48 | tf_op jit(solution)/shard_map/psum | solution.py:88
  442.7 40.8 %all-gather = bf16[32,2,512]{2,1,0:T(2,128)(2,1)S(1)} all-gather(bf16[1,2,512]{2,1,0:T(2,128)(2,1)S(1)} %fusion.29), channel_id=1, replica_groups=mesh['grp'=32,'tp'=8] {'grp'}, dimensions={0}, use_global_device_ids=true | all-gather | bytes 67584 | tf_op jit(solution)/shard_map/all_gather | solution.py:82
  484.4 28.9 %all-reduce.2 = (f32[2]{0:T(128)S(1)}, f32[2,8]{1,0:T(2,128)S(1)}) all-reduce(f32[2]{0:T(128)S(1)} %get-tuple-element.32, f32[2,8]{1,0:T(2,128)S(1)} %bitcast.74), channel_id=1, replica_groups=mesh['grp'=32,'tp'=8] {'tp'}, use_global_device_ids=true, to_apply=%region_11.12 | all-reduce | flops 18 | bytes 144 | tf_op jit(solution)/shard_map/psum | solution.py:95
  514.4 24.8 %all-reduce.1 = (f32[2]{0:T(128)S(1)}, f32[2]{0:T(128)S(1)}) all-reduce(f32[2]{0:T(128)S(1)} %get-tuple-element.13, f32[2]{0:T(128)S(1)} %get-tuple-element.12), channel_id=1, replica_groups=mesh['grp'=32,'tp'=8] {'tp'}, use_global_device_ids=true, to_apply=%region_23.24 | all-reduce | flops 4 | bytes 32 | tf_op jit(solution)/shard_map/psum | solution.py:114
  539.6 28.9 %all-reduce = (f32[128]{0:T(128)S(1)}, f32[256]{0:T(256)S(1)}) all-reduce(f32[128]{0:T(128)S(1)} %fusion.3, f32[256]{0:T(256)S(1)} %fusion), channel_id=1, replica_groups=mesh['grp'=32,'tp'=8] {'tp'}, use_global_device_ids=true, to_apply=%region_25.26 | all-reduce | flops 384 | bytes 3072 | tf_op jit(solution)/shard_map/psum | solution.py:123
  568.6 1.3 fusion.17
  570.2 4.5 add_bitcast_fusion
  574.8 68.1 %psum.99 = f32[]{:T(128)} all-reduce(f32[]{:T(128)} %get-tuple-element.36), channel_id=1, replica_groups=mesh['grp'=32,'tp'=8] {'grp'}, use_global_device_ids=true, to_apply=%region_21.22 | all-reduce | flops 1 | bytes 8 | tf_op jit(solution)/shard_map/psum | solution.py:107
  644.2 82.5 %reduce-scatter.2.cloned.1.call-done = f32[128,512]{0,1:T(8,128)} async-done(((f32[4096,512]{0,1:T(8,128)}), f32[128,512]{0,1:T(8,128)}) %reduce-scatter.2.cloned.1.call-update) | async-done | bytes 262160 | tf_op jit(solution)/shard_map/reduce_scatter | solution.py:128
  726.7 1.8 copy.17
  (51 shorter events, 9.4 us)
Async XLA Ops:
  7.2 206.0 %copy-start.3 = (bf16[2,128,512]{2,1,0:T(8,128)(2,1)S(1)}, bf16[2,128,512]{2,1,0:T(8,128)(2,1)}, u32[]{:S(2)}) copy-start(bf16[2,128,512]{2,1,0:T(8,128)(2,1)} %param.15) | copy-start | bytes 786436
  7.2 67.4 %all-gather.7.cloned.1.call-start = ((), (), s32[]{:S(2)}) async-start(), calls=%async_computation.1 | async-start | bytes 1179648 | tf_op jit(solution)/shard_map/all_gather | solution.py:53
  7.9 127.5 %all-gather.9.cloned.1.call-start = ((), (), s32[]{:S(2)}) async-start(), calls=%async_computation.2 | async-start | bytes 4325376 | tf_op jit(solution)/shard_map/all_gather | solution.py:59
  8.7 204.5 %all-gather.11.cloned.1.call-start = ((), (), s32[]{:S(2)}) async-start(), calls=%async_computation.3 | async-start | bytes 2359296 | tf_op jit(solution)/shard_map/all_gather | solution.py:54
  9.4 313.8 %all-gather.13.cloned.1.call-start = ((), (), s32[]{:S(2)}) async-start(), calls=%async_computation.4 | async-start | bytes 4718592 | tf_op jit(solution)/shard_map/all_gather | solution.py:51
  10.0 373.9 %all-gather.15.cloned.1.call-start = ((), (), s32[]{:S(2)}) async-start(), calls=%async_computation.5 | async-start | bytes 4325376 | tf_op jit(solution)/shard_map/all_gather | solution.py:58
  10.6 716.1 %reduce-scatter.2.cloned.1.call-start = ((), (), s32[]{:S(2)}) async-start(), calls=%async_computation.6 | async-start | bytes 8650752 | tf_op jit(solution)/shard_map/reduce_scatter | solution.py:128
  138.7 245.2 %copy-start.2 = (bf16[2,256,512]{2,1,0:T(8,128)(2,1)S(1)}, bf16[2,256,512]{2,1,0:T(8,128)(2,1)}, u32[]{:S(2)}) copy-start(bf16[2,256,512]{2,1,0:T(8,128)(2,1)} %param.20) | copy-start | bytes 1572868
  389.7 178.9 %copy-start = (bf16[2,64,4096]{2,1,0:T(8,128)(2,1)S(1)}, bf16[2,64,4096]{2,1,0:T(8,128)(2,1)}, u32[]{:S(2)}) copy-start(bf16[2,64,4096]{2,1,0:T(8,128)(2,1)} %all-gather.7.cloned.1.call-done) | copy-start | bytes 3145732
  568.6 1.6 copy-start.1
Sparse Core Ops, SparseCore 0:
  10.5 64.0 all-gather.6
  76.5 58.8 all-gather.8
  137.9 75.2 all-gather.10
  215.5 107.6 all-gather.12
  324.9 58.8 all-gather.14
  574.9 151.7 reduce-scatter.1
where the time goes:
time: 737 us; the launch traced here: 736 us
  waiting for transfers between devices  446 us (61%)
  blocking collectives  243 us (33%)
  matrix products  19.4 us (3%)
  between operations  16 us (2%)
  other arithmetic  8.61 us (1%)
    all_gather x1, waiting for transfers between devices, shards(): lax.all_gather(pass_attn, 'tp', axis=2, tiled=True)  106 us
    reduce_scatter x1, waiting for transfers between devices, shards(): lax.psum_scatter(contract_rows(query_full, dh_q) + contract_rows(pos_full...  82.5 us
    all_gather x1, waiting for transfers between devices, shards(): lax.all_gather(p_attn, 'tp', axis=2, tiled=True)  74.5 us
    psum x1, blocking collectives, shards(): loss = lax.psum(jnp.sum(terms), 'grp') / (queries * grp_size)  68.1 us
    all_gather x1, waiting for transfers between devices, shards(): piece = lax.all_gather(w_out, 'grp', axis=0, tiled=True)  60.8 us
    all_gather x1, waiting for transfers between devices, shards(): lax.all_gather(w_snap, 'grp', axis=0, tiled=True)  60.6 us
    all_gather x1, waiting for transfers between devices, shards(): lax.all_gather(q_attn, 'tp', axis=2, tiled=True)  58.9 us
    all_gather x1, blocking collectives, shards(): index_all = lax.all_gather(passage_index, 'grp', axis=0, tiled=True)  40.8 us
  transfers between devices with their start and end apart: 6, of which 6 were waited for; matrix products, arithmetic and copies ran while one was open for 2% of the time, Pallas kernels for 0%

commit v1 on v0

--- a/solution.py
+++ b/solution.py
@@ -5,6 +5,18 @@
 
 EPS = 1e-06
 TEMP = 0.05
+
+
+def open_the_desk(local_x, row_dim):
+    return jnp.concatenate(
+        lax.all_to_all(
+            jnp.stack([local_x] * lax.axis_size("grp"), 0),
+            axis_name="grp",
+            split_axis=0,
+            concat_axis=0,
+        ),
+        row_dim,
+    )
 
 
 def add_block(tokens, piece):
@@ -55,7 +67,7 @@
     )
     query_full = query_full.reshape(queries * qlen, width)
     pos_full = pos_full.reshape(queries * poslen, width)
-    proj_s = add_block(pass_full, lax.all_gather(w_snap, "grp", axis=0, tiled=True))
+    proj_s = add_block(pass_full, open_the_desk(w_snap, 0))
     piece = lax.all_gather(w_out, "grp", axis=0, tiled=True)
     proj_q = add_block(query_full, piece)
     proj_p = add_block(pos_full, piece)

time: 737 us -> 704 us (0.955)
  waiting for transfers between devices: 446 us -> 408 us
  starting transfers between devices: 0.23 us -> 9.22 us
    all_gather x1 -> x0, waiting for transfers between devices: 60.6 us -> none  [shards(): lax.all_gather(w_snap, 'grp', axis=0, tiled=True)]
    all_gather x1, waiting for transfers between devices: 60.8 us -> 79 us  [shards(): piece = lax.all_gather(w_out, 'grp', axis=0, tiled=True)]
    all_to_all x0 -> x1, starting transfers between devices: none -> 9.02 us  [open_the_desk(): lax.all_to_all(jnp.stack([local_x] * lax.axis_size('grp'), 0), axis_name=...]
  transfers between devices with their start and end apart: 6 -> 6, of which waited for: 6 -> 5; matrix products, arithmetic and copies ran while one was open for 2% -> 2% of each run, Pallas kernels for 0% -> 0%
where the time goes in v1:
time: 704 us; the launch traced here: 703 us
  waiting for transfers between devices  408 us (58%)
  blocking collectives  241 us (34%)
  matrix products  19.5 us (3%)
  between operations  15.7 us (2%)
  starting transfers between devices  9.22 us (1%)
    all_gather x1, waiting for transfers between devices, shards(): lax.all_gather(pass_attn, 'tp', axis=2, tiled=True)  108 us
    reduce_scatter x1, waiting for transfers between devices, shards(): lax.psum_scatter(contract_rows(query_full, dh_q) + contract_rows(pos_full...  83.6 us
    all_gather x1, waiting for transfers between devices, shards(): lax.all_gather(p_attn, 'tp', axis=2, tiled=True)  80.8 us
    all_gather x1, waiting for transfers between devices, shards(): piece = lax.all_gather(w_out, 'grp', axis=0, tiled=True)  79 us
    psum x1, blocking collectives, shards(): loss = lax.psum(jnp.sum(terms), 'grp') / (queries * grp_size)  68 us
    all_gather x1, waiting for transfers between devices, shards(): lax.all_gather(q_attn, 'tp', axis=2, tiled=True)  53.8 us
    all_gather x1, blocking collectives, shards(): index_all = lax.all_gather(passage_index, 'grp', axis=0, tiled=True)  39.6 us
    psum x1, blocking collectives, shards(): lax.psum((jnp.sum(pooled_q * pooled_q, axis=1), jnp.sum(pooled_p * pooled...  28.9 us
  transfers between devices with their start and end apart: 6, of which 5 were waited for; matrix products, arithmetic and copies ran while one was open for 2% of the time, Pallas kernels for 0%

profile of v1, /device:TPU:24, one launch (start us, length us, event | category | flops | bytes accessed | tf_op | source)
XLA Modules:
  0.0 703.2 jit_solution(9942183420980986301)
XLA Ops:
  7.2 0.7 all-gather.10.cloned.1.call-update
  7.9 0.7 all-gather.8.cloned.1.call-update
  8.7 0.7 all-gather.12.cloned.1.call-update
  9.4 3.3 stack.2
  12.7 9.0 %all-to-all-start = ((bf16[32,128,512]{2,1,0:T(8,128)(2,1)}), bf16[32,128,512]{2,1,0:T(8,128)(2,1)}, u32[]{:S(2)}, u32[]{:S(2)}) async-start(bf16[32,128,512]{2,1,0:T(8,128)(2,1)} %stack.2), calls=%async_computation | async-start | bytes 8388608 | tf_op jit(solution)/shard_map/all_to_all | solution.py:12
  22.9 80.8 %all-gather.10.cloned.1.call-done = bf16[2,128,4096]{2,1,0:T(8,128)(2,1)} async-done(((bf16[2,128,512]{2,1,0:T(8,128)(2,1)}), bf16[2,128,4096]{2,1,0:T(8,128)(2,1)}) %all-gather.10.cloned.1.call-update) | async-done | bytes 2097168 | tf_op jit(solution)/shard_map/all_gather | solution.py:66
  103.7 79.0 %all-gather.8.cloned.1.call-done = bf16[4096,512]{1,0:T(8,128)(2,1)} async-done(((bf16[128,512]{1,0:T(8,128)(2,1)}), bf16[4096,512]{1,0:T(8,128)(2,1)}) %all-gather.8.cloned.1.call-update) | async-done | bytes 4194320 | tf_op jit(solution)/shard_map/all_gather | solution.py:71
  182.7 4.1 multiply_reduce_fusion.2
  186.9 108.1 %all-gather.12.cloned.1.call-done = bf16[2,256,4096]{2,1,0:T(8,128)(2,1)} async-done(((bf16[2,256,512]{2,1,0:T(8,128)(2,1)}), bf16[2,256,4096]{2,1,0:T(8,128)(2,1)}) %all-gather.12.cloned.1.call-update) | async-done | bytes 4194320 | tf_op jit(solution)/shard_map/all_gather | solution.py:63
  295.0 5.9 multiply_reduce_fusion.1
  300.9 53.8 %all-gather.6.cloned.1.call-done = bf16[2,64,4096]{2,1,0:T(8,128)(2,1)} async-done(((bf16[2,64,512]{2,1,0:T(8,128)(2,1)}), bf16[2,64,4096]{2,1,0:T(8,128)(2,1)}) %all-gather.6.cloned.1.call-update) | async-done | bytes 1048592 | tf_op jit(solution)/shard_map/all_gather | solution.py:65
  354.7 3.4 multiply_reduce_fusion.3
  358.1 21.7 %all-reduce.4 = (f32[256]{0:T(256)S(1)}, f32[128]{0:T(128)S(1)}, f32[512]{0:T(512)S(1)}) all-reduce(f32[256]{0:T(256)S(1)} %get-tuple-element.42, f32[128]{0:T(128)S(1)} %get-tuple-element.44, f32[512]{0:T(512)S(1)} %get-tuple-element.46), channel_id=1, replica_groups=mesh['grp'=32,'tp'=8] {'tp'}, use_global_device_ids=true, to_apply=%region_6.0 | all-reduce | flops 896 | bytes 7168 | tf_op jit(solution)/shard_map/psum | solution.py:87
  380.8 28.9 %all-reduce.3 = (f32[2]{0:T(128)S(1)}, f32[2]{0:T(128)S(1)}, f32[2]{0:T(128)S(1)}) all-reduce(f32[2]{0:T(128)S(1)} %multiply_reduce_fusion.8, f32[2]{0:T(128)S(1)} %multiply_reduce_fusion.9, f32[2]{0:T(128)S(1)} %get-tuple-element.27), channel_id=1, replica_groups=mesh['grp'=32,'tp'=8] {'tp'}, use_global_device_ids=true, to_apply=%region_9.0 | all-reduce | flops 6 | bytes 48 | tf_op jit(solution)/shard_map/psum | solution.py:100
  409.8 39.6 %all-gather = bf16[32,2,512]{2,1,0:T(2,128)(2,1)S(1)} all-gather(bf16[1,2,512]{2,1,0:T(2,128)(2,1)S(1)} %fusion.29), channel_id=1, replica_groups=mesh['grp'=32,'tp'=8] {'grp'}, dimensions={0}, use_global_device_ids=true | all-gather | bytes 67584 | tf_op jit(solution)/shard_map/all_gather | solution.py:94
  450.3 28.7 %all-reduce.2 = (f32[2]{0:T(128)S(1)}, f32[2,8]{1,0:T(2,128)S(1)}) all-reduce(f32[2]{0:T(128)S(1)} %get-tuple-element.32, f32[2,8]{1,0:T(2,128)S(1)} %bitcast.75), channel_id=1, replica_groups=mesh['grp'=32,'tp'=8] {'tp'}, use_global_device_ids=true, to_apply=%region_11.12 | all-reduce | flops 18 | bytes 144 | tf_op jit(solution)/shard_map/psum | solution.py:107
  480.2 24.9 %all-reduce.1 = (f32[2]{0:T(128)S(1)}, f32[2]{0:T(128)S(1)}) all-reduce(f32[2]{0:T(128)S(1)} %get-tuple-element.13, f32[2]{0:T(128)S(1)} %get-tuple-element.12), channel_id=1, replica_groups=mesh['grp'=32,'tp'=8] {'tp'}, use_global_device_ids=true, to_apply=%region_23.24 | all-reduce | flops 4 | bytes 32 | tf_op jit(solution)/shard_map/psum | solution.py:126
  505.6 28.7 %all-reduce = (f32[128]{0:T(128)S(1)}, f32[256]{0:T(256)S(1)}) all-reduce(f32[128]{0:T(128)S(1)} %fusion.3, f32[256]{0:T(256)S(1)} %fusion), channel_id=1, replica_groups=mesh['grp'=32,'tp'=8] {'tp'}, use_global_device_ids=true, to_apply=%region_25.26 | all-reduce | flops 384 | bytes 3072 | tf_op jit(solution)/shard_map/psum | solution.py:135
  534.6 1.3 fusion.17
  536.2 4.5 add_bitcast_fusion
  540.8 68.0 %psum.99 = f32[]{:T(128)} all-reduce(f32[]{:T(128)} %get-tuple-element.36), channel_id=1, replica_groups=mesh['grp'=32,'tp'=8] {'grp'}, use_global_device_ids=true, to_apply=%region_21.22 | all-reduce | flops 1 | bytes 8 | tf_op jit(solution)/shard_map/psum | solution.py:119
  609.5 0.7 multiply_convert_fusion
  610.1 83.6 %reduce-scatter.2.cloned.1.call-done = f32[128,512]{0,1:T(8,128)} async-done(((f32[4096,512]{0,1:T(8,128)}), f32[128,512]{0,1:T(8,128)}) %reduce-scatter.2.cloned.1.call-update) | async-done | bytes 262160 | tf_op jit(solution)/shard_map/reduce_scatter | solution.py:140
  693.7 1.8 copy.17
  (61 shorter events, 5.3 us)
Async XLA Ops:
  7.2 96.5 %all-gather.10.cloned.1.call-start = ((), (), s32[]{:S(2)}) async-start(), calls=%async_computation.4 | async-start | bytes 2359296 | tf_op jit(solution)/shard_map/all_gather | solution.py:66
  7.9 174.8 %all-gather.8.cloned.1.call-start = ((), (), s32[]{:S(2)}) async-start(), calls=%async_computation.3 | async-start | bytes 4325376 | tf_op jit(solution)/shard_map/all_gather | solution.py:71
  8.6 286.3 %all-gather.12.cloned.1.call-start = ((), (), s32[]{:S(2)}) async-start(), calls=%async_computation.5 | async-start | bytes 4718592 | tf_op jit(solution)/shard_map/all_gather | solution.py:63
  12.7 9.7 %copy-start.4 = (s32[2,8]{1,0:T(2,128)S(1)}, s32[2,8]{1,0:T(2,128)}, u32[]{:S(2)}) copy-start(s32[2,8]{1,0:T(2,128)} %param.23) | copy-start | bytes 196
  12.7 9.7 %copy-start.5 = (s32[32]{0:T(128)S(1)}, s32[32]{0:T(128)}, u32[]{:S(2)}) copy-start(s32[32]{0:T(128)} %param.22) | copy-start | bytes 388
  12.7 10.0 %copy-start.3 = (bf16[512]{0:T(512)(128)(2,1)S(1)}, bf16[512]{0:T(512)(128)(2,1)}, u32[]{:S(2)}) copy-start(bf16[512]{0:T(512)(128)(2,1)} %param.18) | copy-start | bytes 3076
  12.7 10.0 %copy-start.6 = (s32[2]{0:T(128)S(1)}, s32[2]{0:T(128)}, u32[]{:S(2)}) copy-start(s32[2]{0:T(128)} %param.21) | copy-start | bytes 28
  12.7 170.0 %copy-start.8 = (bf16[2,128,512]{2,1,0:T(8,128)(2,1)S(1)}, bf16[2,128,512]{2,1,0:T(8,128)(2,1)}, u32[]{:S(2)}) copy-start(bf16[2,128,512]{2,1,0:T(8,128)(2,1)} %param.15) | copy-start | bytes 786436
  12.7 282.3 %all-to-all-start = ((bf16[32,128,512]{2,1,0:T(8,128)(2,1)}), bf16[32,128,512]{2,1,0:T(8,128)(2,1)}, u32[]{:S(2)}, u32[]{:S(2)}) async-start(bf16[32,128,512]{2,1,0:T(8,128)(2,1)} %stack.2), calls=%async_computation | async-start | bytes 8388608 | tf_op jit(solution)/shard_map/all_to_all | solution.py:12
  21.8 273.2 %copy-start.7 = (bf16[2,256,512]{2,1,0:T(8,128)(2,1)S(1)}, bf16[2,256,512]{2,1,0:T(8,128)(2,1)}, u32[]{:S(2)}) copy-start(bf16[2,256,512]{2,1,0:T(8,128)(2,1)} %param.20) | copy-start | bytes 1572868
  21.8 332.9 %all-gather.6.cloned.1.call-start = ((), (), s32[]{:S(2)}) async-start(), calls=%async_computation.2 | async-start | bytes 1179648 | tf_op jit(solution)/shard_map/all_gather | solution.py:65
  22.4 671.3 %reduce-scatter.2.cloned.1.call-start = ((), (), s32[]{:S(2)}) async-start(), calls=%async_computation.6 | async-start | bytes 8650752 | tf_op jit(solution)/shard_map/reduce_scatter | solution.py:140
  295.0 59.7 %copy-start.2 = (bf16[2,64,512]{2,1,0:T(8,128)(2,1)S(1)}, bf16[2,64,512]{2,1,0:T(8,128)(2,1)}, u32[]{:S(2)}) copy-start(bf16[2,64,512]{2,1,0:T(8,128)(2,1)} %param.13) | copy-start | bytes 393220
  354.7 179.9 %copy-start = (bf16[2,64,4096]{2,1,0:T(8,128)(2,1)S(1)}, bf16[2,64,4096]{2,1,0:T(8,128)(2,1)}, u32[]{:S(2)}) copy-start(bf16[2,64,4096]{2,1,0:T(8,128)(2,1)} %all-gather.6.cloned.1.call-done) | copy-start | bytes 3145732
  534.6 1.6 copy-start.1
Sparse Core Ops, SparseCore 0:
  10.5 93.1 all-gather.9
  105.5 77.1 all-gather.7
  185.2 109.7 all-gather.11
  297.3 57.3 all-gather.5
  540.9 152.7 reduce-scatter.1
